TPU v7x, 128 devices: a whole 4x4x4 slice. The times are simulated.
128 devices in a mesh: dp: 128 (over y, x, z, core).
Axes of the slice: x: 4, y: 4, z: 4, core: 2. Of those that a mesh axis runs over, the one named last changes fastest.
Arguments:
- queries: bfloat16 [65536, 4096], P('dp'), may hold values from -16 to 16
- passages: bfloat16 [65536, 4096], P('dp'), may hold values from -16 to 16
- links: int32 [128, 3], P('dp'), may hold values 0 or 1
- positives: int32 [128, 512], P('dp'), may hold values from 0 to 511, each once within a row
Outputs:
- query_grad: bfloat16 [65536, 4096], P('dp')
- passage_grad: bfloat16 [65536, 4096], P('dp')
- row_loss: float32 [65536], P('dp')
- col_loss: float32 [65536], P('dp')
All inputs are finite; a program needn't handle non-finite values. No bound on the sum of `links` on one device may be relied on, other than what follows from the above.
Results may differ from a plain program's by a relative error of at most 0.0048.
Values may be sent and summed in bfloat16 or wider, within the bound.
A program may use at most 192 MiB of HBM per device.

v0:
```python
import jax
import jax.numpy as jnp
from jax import lax
from jax.sharding import PartitionSpec as P


def passed_along(block, axis, distance):
    devices = range(lax.axis_size(axis))
    route = [((i - distance) % len(devices), i) for i in devices]
    return lax.ppermute(block, axis, route)


def local(queries, passages, links, positives):
    count = queries.shape[0]
    factor = queries.shape[1] ** (-0.5)
    hop_count = links.shape[1]
    floor_value = -1e30

    def scores_of(block):
        return jnp.einsum("rd,cd->rc", queries, block, preferred_element_type=jnp.float32) * factor

    def masked_scores(block):
        return jnp.full((count, count), floor_value, jnp.float32)

    columns = lax.broadcasted_iota(jnp.int32, (count, count), 1)
    matches = (positives[0][:, None] == columns).astype(jnp.float32)
    diagonal = scores_of(passages)
    fetched = []
    tiles = []
    flags = []
    first_max = jnp.max(diagonal, axis=0)
    col_maxima = [first_max]
    col_sums = [jnp.sum(jnp.exp(diagonal - first_max[None, :]), axis=0)]
    for offset in range(1, hop_count + 1):
        remote = passed_along(passages, "dp", -offset)
        flag = links[0, offset - 1] > 0
        tile = lax.cond(flag, scores_of, masked_scores, remote)
        part_max = jnp.max(tile, axis=0)
        part_sum = jnp.sum(jnp.exp(tile - part_max[None, :]), axis=0) * flag.astype(jnp.float32)
        back_max, back_sum = passed_along((part_max, part_sum), "dp", offset)
        col_maxima.append(back_max)
        col_sums.append(back_sum)
        tiles.append(tile)
        flags.append(flag)
        fetched.append(remote)
    stacked = jnp.stack([diagonal] + tiles)
    row_max = jnp.max(stacked, axis=(0, 2))
    row_lse = row_max + jnp.log(jnp.sum(jnp.exp(stacked - row_max[None, :, None]), axis=(0, 2)))
    maxima = jnp.stack(col_maxima)
    col_top = jnp.max(maxima, axis=0)
    col_lse = col_top + jnp.log(
        jnp.sum(jnp.stack(col_sums) * jnp.exp(maxima - col_top[None, :]), axis=0)
    )

    def tile_grads(operands):
        tile, block, remote_lse = operands
        weights = (jnp.exp(tile - row_lse[:, None]) + jnp.exp(tile - remote_lse[None, :])).astype(
            jnp.bfloat16
        )
        query_term = (
            jnp.einsum("rc,cd->rd", weights, block, preferred_element_type=jnp.float32) * factor
        )
        passage_term = (
            jnp.einsum("rc,rd->cd", weights, queries, preferred_element_type=jnp.float32) * factor
        )
        return (query_term, passage_term)

    def no_grads(operands):
        empty = jnp.zeros(queries.shape, jnp.float32)
        return (empty, empty)

    diag_weights = (
        jnp.exp(diagonal - row_lse[:, None]) + jnp.exp(diagonal - col_lse[None, :]) - 2.0 * matches
    ).astype(jnp.bfloat16)
    query_grad = (
        jnp.einsum("rc,cd->rd", diag_weights, passages, preferred_element_type=jnp.float32) * factor
    )
    passage_grad = (
        jnp.einsum("rc,rd->cd", diag_weights, queries, preferred_element_type=jnp.float32) * factor
    )
    for offset in range(1, hop_count + 1):
        remote_lse = passed_along(col_lse, "dp", -offset)
        block = fetched[offset - 1]
        query_term, passage_term = lax.cond(
            flags[offset - 1], tile_grads, no_grads, (tiles[offset - 1], block, remote_lse)
        )
        query_grad = query_grad + query_term
        returned = passed_along(passage_term.astype(jnp.bfloat16), "dp", offset)
        passage_grad = passage_grad + returned.astype(jnp.float32)
    row_loss = row_lse - jnp.sum(matches * diagonal, axis=1)
    col_loss = col_lse - jnp.sum(matches * diagonal, axis=0)
    return (query_grad.astype(jnp.bfloat16), passage_grad.astype(jnp.bfloat16), row_loss, col_loss)


def solution(mesh):
    placed = (P("dp", None), P("dp", None), P("dp", None), P("dp", None))
    return jax.shard_map(
        local,
        mesh=mesh,
        in_specs=placed,
        out_specs=(P("dp", None), P("dp", None), P("dp"), P("dp")),
        check_vma=False,
    )
```

profile of v0, /device:TPU:32, one launch (start us, length us, event | category | flops | bytes accessed | tf_op | source)
XLA Modules:
  0.0 613.8 jit_solution(6214100406353935648)
XLA Ops:
  0.7 8.2 %collective-permute-start.1 = (bf16[512,4096]{1,0:T(8,128)(2,1)}, bf16[512,4096]{1,0:T(8,128)(2,1)}, u32[]{:S(2)}, u32[]{:S(2)}) collective-permute-start(bf16[512,4096]{1,0:T(8,128)(2,1)} %param.17), channel_id=1, source_target_pairs={{2,0},{3,1},{4,2},{5,3},{6,4},{7,5},{8,6},{9,7},{10,8},{11,9},{12,... | collective-permute-start | bytes 12582920 | tf_op jit(solution)/shard_map/ppermute | solution.py:10
  8.9 1.4 fusion.14
  12.3 6.0 fusion.15
  18.7 118.2 %collective-permute-done = bf16[512,4096]{1,0:T(8,128)(2,1)} collective-permute-done((bf16[512,4096]{1,0:T(8,128)(2,1)}, bf16[512,4096]{1,0:T(8,128)(2,1)}, u32[]{:S(2)}, u32[]{:S(2)}) %collective-permute-start) | collective-permute-done | bytes 4194336 | tf_op jit(solution)/shard_map/ppermute | solution.py:10
  136.9 7.0 %conditional.6 = (f32[512,512]{1,0:T(8,128)}, f32[1,512,512]{2,1,0:T(8,128)S(1)}, f32[512]{0:T(512)S(1)}, f32[512]{0:T(512)S(1)}) conditional(s32[]{:T(128)} %bitcast.3, () %tuple.62, (bf16[512,4096]{1,0:T(8,128)(2,1)S(1)}, bf16[512,4096]{1,0:T(8,128)(2,1)}) %tuple.101), branch_computations={%region_1.0_spmd, %region_2.5_spmd} | conditional | flops 2148269056 | bytes 11538464 | solution.py:37
  136.9 5.8 fusion.9
  142.7 1.2 copy.29
  143.9 82.7 %collective-permute-done.1 = bf16[512,4096]{1,0:T(8,128)(2,1)} collective-permute-done((bf16[512,4096]{1,0:T(8,128)(2,1)}, bf16[512,4096]{1,0:T(8,128)(2,1)}, u32[]{:S(2)}, u32[]{:S(2)}) %collective-permute-start.1) | collective-permute-done | bytes 4194336 | tf_op jit(solution)/shard_map/ppermute | solution.py:10
  226.6 8.0 %conditional.7 = (f32[512,512]{1,0:T(8,128)}, f32[1,512,512]{2,1,0:T(8,128)S(1)}, f32[512]{0:T(512)S(1)}, f32[512]{0:T(512)S(1)}) conditional(s32[]{:T(128)} %bitcast.4, () %tuple.64, (bf16[512,4096]{1,0:T(8,128)(2,1)}, bf16[512,4096]{1,0:T(8,128)(2,1)}) %tuple.65), branch_computations={%region_5.0_spmd, %region_6.9_spmd} | conditional | flops 2148269056 | bytes 11538464 | solution.py:37
  226.6 6.8 %fusion.10 = (f32[512]{0:T(512)S(1)}, f32[512]{0:T(512)S(1)}, f32[512,512]{1,0:T(8,128)}) fusion(bf16[512,4096]{1,0:T(8,128)(2,1)} %get-tuple-element.56, bf16[512,4096]{1,0:T(8,128)(2,1)} %get-tuple-element.57), kind=kOutput, calls=%fused_computation.41 | convolution fusion | flops 2148269056 | bytes 9441280 | tf_op jit(solution)/shard_map/cond/branch_1_fun/rd,cd->rc/dot_general | solution.py:20
  233.4 1.2 copy.21
  234.7 1.2 conditional.8
  234.7 1.1 broadcast.56
  235.9 43.0 %collective-permute-start.5 = (f32[512]{0:T(512)S(1)}, f32[512]{0:T(512)S(1)}, u32[]{:S(2)}, u32[]{:S(2)}) collective-permute-start(f32[512]{0:T(512)S(1)} %get-tuple-element.105), channel_id=1, source_target_pairs={{125,0},{126,1},{127,2},{0,3},{1,4},{2,5},{3,6},{4,7},{5,8},{6,9},... | collective-permute-start | bytes 6152 | tf_op jit(solution)/shard_map/ppermute | solution.py:10
  278.9 1.4 exponential_reduce_fusion.1
  280.6 1.4 exponential_reduce_fusion
  282.3 1.4 exponential_reduce_fusion.2
  283.7 1.0 fusion.1
  284.7 0.8 collective-permute-start.6
  285.5 5.3 collective-permute-done.8
  290.9 0.6 fusion.12
  291.5 2.2 collective-permute-start.9
  293.6 7.3 %collective-permute-start.10 = (f32[512]{0:T(512)S(1)}, f32[512]{0:T(512)S(1)}, u32[]{:S(2)}, u32[]{:S(2)}) collective-permute-start(f32[512]{0:T(512)S(1)} %get-tuple-element.126), channel_id=1, source_target_pairs={{2,0},{3,1},{4,2},{5,3},{6,4},{7,5},{8,6},{9,7},{10,8},{11,9},{12,... | collective-permute-start | bytes 6152 | tf_op jit(solution)/shard_map/ppermute | solution.py:10
  300.9 3.4 collective-permute-start.11
  304.9 8.8 %conditional.9 = (f32[512,4096]{1,0:T(8,128)S(1)}, f32[512,4096]{1,0:T(8,128)S(1)}) conditional(s32[]{:T(128)} %bitcast.3, () %tuple.68, (f32[512]{0:T(512)S(1)}, f32[512,512]{1,0:T(8,128)}, f32[512]{0:T(512)S(1)}, bf16[512,4096]{1,0:T(8,128)(2,1)}, bf16[512,4096]{1,0:T(8,128)(2,1)S(1)}) %tuple.102), branch_computations={%region_20.0_spmd, %region_21.0_spmd} | conditional | flops 4301258752 | bytes 27271184 | solution.py:84
  304.9 3.8 convolution_multiply_fusion.3
  308.8 5.0 convolution_multiply_fusion.4
  313.7 3.2 copy-done.5
  316.9 3.2 copy-done.6
  320.2 6.1 convert_element_type.81
  326.3 12.3 %conditional.10 = (f32[512,4096]{1,0:T(8,128)S(1)}, f32[512,4096]{1,0:T(8,128)}) conditional(s32[]{:T(128)} %bitcast.4, () %tuple.70, (f32[512]{0:T(512)S(1)}, f32[512,512]{1,0:T(8,128)}, f32[512]{0:T(512)S(1)}, bf16[512,4096]{1,0:T(8,128)(2,1)}, bf16[512,4096]{1,0:T(8,128)(2,1)S(1)}) %tuple.103), branch_computations={%region_22.0_spmd, %region_23.0_spmd} | conditional | flops 4301258752 | bytes 27271184 | solution.py:84
  326.5 7.1 %convolution_multiply_fusion.5 = f32[512,4096]{1,0:T(8,128)} fusion(bf16[512,4096]{1,0:T(8,128)(2,1)S(1)} %get-tuple-element.69, f32[512,512]{1,0:T(8,128)} %get-tuple-element.65, f32[512]{0:T(512)S(1)} %get-tuple-element.67, f32[512]{0:T(512)S(1)} %get-tuple-element.66), kind=kOutput, calls=%fused_computation.6 | convolution fusion | flops 2150629376 | bytes 13635584 | tf_op jit(solution)/shard_map/cond/branch_1_fun/rc,rd->cd/dot_general | solution.py:64
  333.6 5.0 convolution_multiply_fusion.6
  338.6 3.2 copy-done.7
  341.8 6.1 convert_element_type.83
  347.9 0.9 collective-permute-start.13
  348.8 5.3 conditional.11
  348.8 1.0 broadcast.62
  349.8 4.2 broadcast.62.clone
  354.1 3.2 copy-done.8
  357.3 6.2 %convert_element_type.85 = bf16[512,4096]{1,0:T(8,128)(2,1)} convert(f32[512,4096]{1,0:T(8,128)} %get-tuple-element.114) | non-fusion elementwise | flops 2097152 | bytes 12582912 | tf_op jit(solution)/shard_map/convert_element_type | solution.py:88
  363.8 2.7 fusion.7
  366.5 5.8 fusion.8
  372.3 14.4 %add_convert_fusion.10 = bf16[512,4096]{1,0:T(8,128)(2,1)} fusion(f32[512,4096]{1,0:T(8,128)} %copy-done.8, f32[512,4096]{1,0:T(8,128)} %copy-done.7, f32[512,4096]{1,0:T(8,128)} %copy-done.6, f32[512,4096]{1,0:T(8,128)} %fusion.8), kind=kLoop, calls=%fused_computation.13 | loop fusion | flops 10485760 | bytes 37748736 | tf_op jit(solution)/shard_map/convert_element_type | solution.py:92
  386.7 10.5 %collective-permute-done.12 = bf16[512,4096]{1,0:T(8,128)(2,1)} collective-permute-done((bf16[512,4096]{1,0:T(8,128)(2,1)}, bf16[512,4096]{1,0:T(8,128)(2,1)}, u32[]{:S(2)}, u32[]{:S(2)}) %collective-permute-start.12) | collective-permute-done | bytes 4194336 | tf_op jit(solution)/shard_map/ppermute | solution.py:10
  397.2 44.6 %collective-permute-done.13 = bf16[512,4096]{1,0:T(8,128)(2,1)} collective-permute-done((bf16[512,4096]{1,0:T(8,128)(2,1)}, bf16[512,4096]{1,0:T(8,128)(2,1)}, u32[]{:S(2)}, u32[]{:S(2)}) %collective-permute-start.13) | collective-permute-done | bytes 4194336 | tf_op jit(solution)/shard_map/ppermute | solution.py:10
  441.8 164.3 %collective-permute-done.14 = bf16[512,4096]{1,0:T(8,128)(2,1)} collective-permute-done((bf16[512,4096]{1,0:T(8,128)(2,1)}, bf16[512,4096]{1,0:T(8,128)(2,1)}, u32[]{:S(2)}, u32[]{:S(2)}) %collective-permute-start.14) | collective-permute-done | bytes 4194336 | tf_op jit(solution)/shard_map/ppermute | solution.py:10
  606.1 7.3 %add_convert_fusion.9 = bf16[512,4096]{1,0:T(8,128)(2,1)} fusion(bf16[512,4096]{1,0:T(8,128)(2,1)} %collective-permute-done.14, bf16[512,4096]{1,0:T(8,128)(2,1)} %collective-permute-done.13, bf16[512,4096]{1,0:T(8,128)(2,1)} %collective-permute-done.12, f32[512,4096]{1,0:T(8,128)S(1)} %fusion.7), kind=kLoop, calls=%fused_computation.12 | loop fusion | flops 16777216 | bytes 25165824 | tf_op jit(solution)/shard_map/convert_element_type | solution.py:92
  (46 shorter events, 2.1 us)
Async XLA Ops:
  0.6 136.3 %collective-permute-start = (bf16[512,4096]{1,0:T(8,128)(2,1)}, bf16[512,4096]{1,0:T(8,128)(2,1)}, u32[]{:S(2)}, u32[]{:S(2)}) collective-permute-start(bf16[512,4096]{1,0:T(8,128)(2,1)} %param.17), channel_id=1, source_target_pairs={{1,0},{2,1},{3,2},{4,3},{5,4},{6,5},{7,6},{8,7},{9,8},{10,9},{11,1... | collective-permute-start | bytes 12582920 | tf_op jit(solution)/shard_map/ppermute | solution.py:10
  0.7 225.9 %collective-permute-start.1 = (bf16[512,4096]{1,0:T(8,128)(2,1)}, bf16[512,4096]{1,0:T(8,128)(2,1)}, u32[]{:S(2)}, u32[]{:S(2)}) collective-permute-start(bf16[512,4096]{1,0:T(8,128)(2,1)} %param.17), channel_id=1, source_target_pairs={{2,0},{3,1},{4,2},{5,3},{6,4},{7,5},{8,6},{9,7},{10,8},{11,9},{12,... | collective-permute-start | bytes 12582920 | tf_op jit(solution)/shard_map/ppermute | solution.py:10
  8.9 225.7 %collective-permute-start.2 = (bf16[512,4096]{1,0:T(8,128)(2,1)}, bf16[512,4096]{1,0:T(8,128)(2,1)}, u32[]{:S(2)}, u32[]{:S(2)}) collective-permute-start(bf16[512,4096]{1,0:T(8,128)(2,1)} %param.17), channel_id=1, source_target_pairs={{3,0},{4,1},{5,2},{6,3},{7,4},{8,5},{9,6},{10,7},{11,8},{12,9},{13... | collective-permute-start | bytes 12582920 | tf_op jit(solution)/shard_map/ppermute | solution.py:10
  12.2 6.0 copy-start.9
  12.3 124.7 %copy-start = (bf16[512,4096]{1,0:T(8,128)(2,1)S(1)}, bf16[512,4096]{1,0:T(8,128)(2,1)}, u32[]{:S(2)}) copy-start(bf16[512,4096]{1,0:T(8,128)(2,1)} %param.16) | copy-start | bytes 12582916
  143.9 140.7 %collective-permute-start.3 = (f32[512]{0:T(512)S(1)}, f32[512]{0:T(512)S(1)}, u32[]{:S(2)}, u32[]{:S(2)}) collective-permute-start(f32[512]{0:T(512)S(1)} %get-tuple-element.103), channel_id=1, source_target_pairs={{127,0},{0,1},{1,2},{2,3},{3,4},{4,5},{5,6},{6,7},{7,8},{8,9},{9,1... | collective-permute-start | bytes 6152 | tf_op jit(solution)/shard_map/ppermute | solution.py:10
  234.7 50.8 %collective-permute-start.4 = (f32[512]{0:T(512)S(1)}, f32[512]{0:T(512)S(1)}, u32[]{:S(2)}, u32[]{:S(2)}) collective-permute-start(f32[512]{0:T(512)S(1)} %get-tuple-element.104), channel_id=1, source_target_pairs={{126,0},{127,1},{0,2},{1,3},{2,4},{3,5},{4,6},{5,7},{6,8},{7,9},{8... | collective-permute-start | bytes 6152 | tf_op jit(solution)/shard_map/ppermute | solution.py:10
  235.9 69.0 %copy-start.1 = (bf16[512,4096]{1,0:T(8,128)(2,1)S(1)}, bf16[512,4096]{1,0:T(8,128)(2,1)}, u32[]{:S(2)}) copy-start(bf16[512,4096]{1,0:T(8,128)(2,1)} %param.16) | copy-start | bytes 12582916
  235.9 49.6 %collective-permute-start.5 = (f32[512]{0:T(512)S(1)}, f32[512]{0:T(512)S(1)}, u32[]{:S(2)}, u32[]{:S(2)}) collective-permute-start(f32[512]{0:T(512)S(1)} %get-tuple-element.105), channel_id=1, source_target_pairs={{125,0},{126,1},{127,2},{0,3},{1,4},{2,5},{3,6},{4,7},{5,8},{6,9},... | collective-permute-start | bytes 6152 | tf_op jit(solution)/shard_map/ppermute | solution.py:10
  280.4 5.2 collective-permute-start.7
  282.0 8.8 %collective-permute-start.8 = (f32[512]{0:T(512)S(1)}, f32[512]{0:T(512)S(1)}, u32[]{:S(2)}, u32[]{:S(2)}) collective-permute-start(f32[512]{0:T(512)S(1)} %broadcast_multiply_fusion), channel_id=1, source_target_pairs={{125,0},{126,1},{127,2},{0,3},{1,4},{2,5},{3,6},{4,7},{5,8},{6,9},... | collective-permute-start | bytes 6152 | tf_op jit(solution)/shard_map/ppermute | solution.py:10
  284.7 6.2 %collective-permute-start.6 = (f32[512]{0:T(512)S(1)}, f32[512]{0:T(512)S(1)}, u32[]{:S(2)}, u32[]{:S(2)}) collective-permute-start(f32[512]{0:T(512)S(1)} %broadcast_multiply_fusion.2), channel_id=1, source_target_pairs={{127,0},{0,1},{1,2},{2,3},{3,4},{4,5},{5,6},{6,7},{7,8},{8,9},{9,1... | collective-permute-start | bytes 6152 | tf_op jit(solution)/shard_map/ppermute | solution.py:10
  291.5 13.4 %collective-permute-start.9 = (f32[512]{0:T(512)S(1)}, f32[512]{0:T(512)S(1)}, u32[]{:S(2)}, u32[]{:S(2)}) collective-permute-start(f32[512]{0:T(512)S(1)} %get-tuple-element.126), channel_id=1, source_target_pairs={{1,0},{2,1},{3,2},{4,3},{5,4},{6,5},{7,6},{8,7},{9,8},{10,9},{11,1... | collective-permute-start | bytes 6152 | tf_op jit(solution)/shard_map/ppermute | solution.py:10
  293.6 32.7 %collective-permute-start.10 = (f32[512]{0:T(512)S(1)}, f32[512]{0:T(512)S(1)}, u32[]{:S(2)}, u32[]{:S(2)}) collective-permute-start(f32[512]{0:T(512)S(1)} %get-tuple-element.126), channel_id=1, source_target_pairs={{2,0},{3,1},{4,2},{5,3},{6,4},{7,5},{8,6},{9,7},{10,8},{11,9},{12,... | collective-permute-start | bytes 6152 | tf_op jit(solution)/shard_map/ppermute | solution.py:10
  300.9 47.9 %collective-permute-start.11 = (f32[512]{0:T(512)S(1)}, f32[512]{0:T(512)S(1)}, u32[]{:S(2)}, u32[]{:S(2)}) collective-permute-start(f32[512]{0:T(512)S(1)} %get-tuple-element.126), channel_id=1, source_target_pairs={{3,0},{4,1},{5,2},{6,3},{7,4},{8,5},{9,6},{10,7},{11,8},{12,9},{13... | collective-permute-start | bytes 6152 | tf_op jit(solution)/shard_map/ppermute | solution.py:10
  313.7 3.2 copy-start.5
  316.9 3.2 copy-start.6
  320.2 6.1 copy-start.2
  326.3 70.9 %collective-permute-start.12 = (bf16[512,4096]{1,0:T(8,128)(2,1)}, bf16[512,4096]{1,0:T(8,128)(2,1)}, u32[]{:S(2)}, u32[]{:S(2)}) collective-permute-start(bf16[512,4096]{1,0:T(8,128)(2,1)} %convert_element_type.81), channel_id=1, source_target_pairs={{127,0},{0,1},{1,2},{2,3},{3,4},{4,5},{5,6},{6,7},{7,8},{8,9},{9,1... | collective-permute-start | bytes 12582920 | tf_op jit(solution)/shard_map/ppermute | solution.py:10
  338.6 3.2 copy-start.7
  341.8 7.0 %copy-start.3 = (bf16[512,4096]{1,0:T(8,128)(2,1)S(1)}, bf16[512,4096]{1,0:T(8,128)(2,1)}, u32[]{:S(2)}) copy-start(bf16[512,4096]{1,0:T(8,128)(2,1)} %param.16) | copy-start | bytes 12582916
  347.9 93.8 %collective-permute-start.13 = (bf16[512,4096]{1,0:T(8,128)(2,1)}, bf16[512,4096]{1,0:T(8,128)(2,1)}, u32[]{:S(2)}, u32[]{:S(2)}) collective-permute-start(bf16[512,4096]{1,0:T(8,128)(2,1)} %convert_element_type.83), channel_id=1, source_target_pairs={{126,0},{127,1},{0,2},{1,3},{2,4},{3,5},{4,6},{5,7},{6,8},{7,9},{8... | collective-permute-start | bytes 12582920 | tf_op jit(solution)/shard_map/ppermute | solution.py:10
  354.1 3.2 copy-start.8
  357.3 6.4 %copy-start.4 = (bf16[512,4096]{1,0:T(8,128)(2,1)S(1)}, bf16[512,4096]{1,0:T(8,128)(2,1)}, u32[]{:S(2)}) copy-start(bf16[512,4096]{1,0:T(8,128)(2,1)} %param.16) | copy-start | bytes 12582916
  363.5 3.0 copy-start.10
  363.5 242.6 %collective-permute-start.14 = (bf16[512,4096]{1,0:T(8,128)(2,1)}, bf16[512,4096]{1,0:T(8,128)(2,1)}, u32[]{:S(2)}, u32[]{:S(2)}) collective-permute-start(bf16[512,4096]{1,0:T(8,128)(2,1)} %convert_element_type.85), channel_id=1, source_target_pairs={{125,0},{126,1},{127,2},{0,3},{1,4},{2,5},{3,6},{4,7},{5,8},{6,9},... | collective-permute-start | bytes 12582920 | tf_op jit(solution)/shard_map/ppermute | solution.py:10
where the time goes:
time: 619 us; the launch traced here: 614 us
  waiting for transfers between devices  426 us (69%)
  starting transfers between devices  66.6 us (11%)
  matrix products  47.9 us (8%)
  other arithmetic  47 us (8%)
  local copies, waits for them, and re-layouts  23.1 us (4%)
    ppermute x15, waiting for transfers between devices, passed_along(): return lax.ppermute(block, axis, route)  426 us
    ppermute x15, starting transfers between devices, passed_along(): return lax.ppermute(block, axis, route)  66.6 us
    dot_general x3, matrix products, scores_of(): jnp.einsum('rd,cd->rc', queries, block, preferred_element_type=jnp.float32)  18.5 us
    convert_element_type x3, other arithmetic, local(): returned = passed_along(passage_term.astype(jnp.bfloat16), 'dp', offset)  18.4 us
    convert_element_type x1, other arithmetic, local(): query_grad.astype(jnp.bfloat16)  14.4 us
    unnamed x22, local copies, waits for them, and re-layouts  12.9 us
  transfers between devices with their start and end apart: 15, of which 6 were waited for; matrix products, arithmetic and copies ran while one was open for 16% of the time, Pallas kernels for 0%

commit v1 on v0

v1 whole, which is shorter than its diff:
```python
import functools

import jax
import jax.numpy as jnp
from jax import lax
from jax.experimental import pallas as pl
from jax.experimental.pallas import tpu as pltpu
from jax.sharding import PartitionSpec as P

MESH = pl.DeviceIdType.MESH
NEG = -1e30
PIECES = 4
STRIP = 64


def kernel(
    n,
    q_hbm,
    p_hbm,
    links_ref,
    pos_ref,
    dq_hbm,
    dp_hbm,
    row_ref,
    col_ref,
    own,
    far,
    score,
    weight,
    lse,
    stage,
    matches,
    said,
    heard,
    flag_out,
    flag_in,
    load_sem,
    send_sem,
    recv_sem,
    said_sem,
    heard_sem,
    flag_send_sem,
    flag_recv_sem,
    stage_sem,
):
    block, depth = q_hbm.shape
    factor = depth ** (-0.5)
    rows = block // PIECES
    me = lax.axis_index("dp")
    second = lax.rem(me, 2)

    def at(offset):
        return (lax.rem(me + offset + n, n),)

    barrier = pltpu.get_barrier_semaphore()
    for offset in (1, 2, 3, -1, -2, -3):
        pl.semaphore_signal(barrier, inc=1, device_id=at(offset), device_id_type=MESH)
    pl.semaphore_wait(barrier, 6)

    def piece(s):
        return pl.ds(pl.multiple_of(s * rows, rows), rows)

    def send(stream, s, src, slot, offset):
        return pltpu.make_async_remote_copy(
            src_ref=src.at[piece(s)],
            dst_ref=far.at[slot, piece(s)],
            send_sem=send_sem.at[stream, s],
            recv_sem=recv_sem.at[slot, s],
            device_id=at(offset),
            device_id_type=MESH,
        )

    def q_up(s):
        return send(0, s, q_hbm, 4, 2)

    def p_down(s):
        return send(1, s, p_hbm, 1, -2)

    def p_on(s):
        return send(2, s, far.at[1], 2, -1)

    def q_on(s):
        return send(3, s, far.at[4], 5, 1)

    def first_own(s):
        return send(4, s, q_hbm, 3, 1)

    def first_on(s):
        return send(5, s, far.at[1], 0, 1)

    def second_own(s):
        return send(4, s, p_hbm, 0, -1)

    def second_on(s):
        return send(5, s, far.at[4], 3, -1)

    def arrived(slot, s):
        send(0, s, q_hbm, slot, 1).wait_recv()

    def over_pieces(body):
        def step(s, carry):
            body(s)
            return carry

        lax.fori_loop(0, PIECES, step, 0)

    @pl.when(second == 0)
    def _():
        over_pieces(lambda s: p_down(s).start())
        over_pieces(lambda s: first_own(s).start())
        over_pieces(lambda s: q_up(s).start())

    @pl.when(second == 1)
    def _():
        over_pieces(lambda s: q_up(s).start())
        over_pieces(lambda s: p_down(s).start())
        over_pieces(lambda s: second_own(s).start())

    load_q = pltpu.make_async_copy(q_hbm, own.at[0], load_sem.at[0])
    load_p = pltpu.make_async_copy(p_hbm, own.at[1], load_sem.at[1])
    load_q.start()
    load_p.start()

    for k in range(3):
        flag_out[k] = jnp.full((8, 128), links_ref[0, k].astype(jnp.float32), jnp.float32)

    def flag_copy(k):
        return pltpu.make_async_remote_copy(
            src_ref=flag_out.at[k],
            dst_ref=flag_in.at[k],
            send_sem=flag_send_sem.at[k],
            recv_sem=flag_recv_sem.at[k],
            device_id=at(k + 1),
            device_id_type=MESH,
        )

    for k in range(3):
        flag_copy(k).start()

    pos = pos_ref[...].astype(jnp.float32)
    down = lax.broadcasted_iota(jnp.int32, (block, block), 0).astype(jnp.float32)
    matches[1] = (pos == down).astype(jnp.float32)
    upright = jnp.transpose(jnp.broadcast_to(pos, (128, block)))[:, 0:1]
    across = lax.broadcasted_iota(jnp.int32, (block, block), 1).astype(jnp.float32)
    matches[0] = (upright == across).astype(jnp.float32)

    load_q.wait()
    load_p.wait()

    def dot_t(a, b):
        return lax.dot_general(a, b, (((1,), (1,)), ((), ())), preferred_element_type=jnp.float32)

    def diagonal(t, carry):
        side, s = t // PIECES, lax.rem(t, PIECES)
        score[side * 4, :, piece(s)] = dot_t(own[side], own[1 - side, piece(s), :]) * factor
        return carry

    lax.fori_loop(0, 2 * PIECES, diagonal, 0)
    for k in range(3):
        flag_copy(k).wait()

    def score_piece(side, k, s):
        part = dot_t(own[side], far[side * 3 + k - 1, piece(s), :]) * factor
        mine = flag_out[k - 1, 0:1, :]
        theirs = flag_in[k - 1, 0:1, :]
        live = jnp.where(side == 0, mine, theirs)[:, 0:1]
        score[side * 4 + k, :, piece(s)] = jnp.where(live > 0, part, NEG)

    def near(s):
        arrived(1, s)
        p_on(s).start()

        @pl.when(second == 0)
        def _():
            first_on(s).start()

        arrived(4, s)
        q_on(s).start()

        @pl.when(second == 1)
        def _():
            second_on(s).start()

        arrived(0, s)
        arrived(3, s)

        def one(t, carry):
            score_piece(t // 2, lax.rem(t, 2) + 1, s)
            return carry

        lax.fori_loop(0, 4, one, 0)

    over_pieces(near)

    def last(s):
        arrived(2, s)
        arrived(5, s)

        def one(side, carry):
            score_piece(side, 3, s)
            return carry

        lax.fori_loop(0, 2, one, 0)

    over_pieces(last)

    strips = block // STRIP

    def strip(i):
        return pl.ds(pl.multiple_of(i * STRIP, STRIP), STRIP)

    def finish_lse(t, carry):
        side, i = t // strips, lax.rem(t, strips)
        tiles = [score[side * 4 + k, strip(i), :] for k in range(4)]
        top = functools.reduce(jnp.maximum, tiles)
        top = jnp.max(top, axis=1, keepdims=True)
        total = functools.reduce(jnp.add, [jnp.exp(tile - top) for tile in tiles])
        total = jnp.sum(total, axis=1, keepdims=True)
        lse[side, strip(i), :] = jnp.broadcast_to(top + jnp.log(total), (STRIP, 128))
        return carry

    lax.fori_loop(0, 2 * strips, finish_lse, 0)

    def tell(side, k):
        return pltpu.make_async_remote_copy(
            src_ref=said.at[side],
            dst_ref=heard.at[(1 - side) * 3 + k - 1],
            send_sem=said_sem.at[side * 3 + k - 1],
            recv_sem=heard_sem.at[(1 - side) * 3 + k - 1],
            device_id=at(k if side == 0 else -k),
            device_id_type=MESH,
        )

    for side in range(2):
        said[side] = jnp.transpose(lse[side])[0:8, :]
        for k in (1, 2, 3):
            tell(side, k).start()

    row_ref[...] = said[0, 0:1, :] - jnp.sum(matches[1] * score[4], axis=0, keepdims=True)
    col_ref[...] = said[1, 0:1, :] - jnp.sum(matches[0] * score[0], axis=0, keepdims=True)

    def weigh(side, k, i):
        tile = score[side * 4 + k, strip(i), :]
        theirs = said[1 - side, 0:1, :] if k == 0 else heard[side * 3 + k - 1, 0:1, :]
        value = jnp.exp(tile - lse[side, strip(i), 0:1]) + jnp.exp(tile - theirs)
        if k == 0:
            value = value - 2.0 * matches[side, strip(i), :]
        weight[side * 4 + k, strip(i), :] = value.astype(jnp.bfloat16)

    def weigh_diagonal(t, carry):
        weigh(0, 0, t)
        weigh(1, 0, t)
        return carry

    lax.fori_loop(0, strips, weigh_diagonal, 0)
    for side in range(2):
        for k in (1, 2, 3):
            tell(side, k).wait_send()
            tell(side, k).wait_recv()

    def weigh_far(t, carry):
        for side in range(2):
            for k in (1, 2, 3):
                weigh(side, k, t)
        return carry

    lax.fori_loop(0, strips, weigh_far, 0)

    width = stage.shape[2]
    parts = depth // width

    def out_copy(side, j):
        hbm = dq_hbm if side == 0 else dp_hbm
        return pltpu.make_async_copy(
            stage.at[lax.rem(j, 2)],
            hbm.at[:, pl.ds(pl.multiple_of(j * width, width), width)],
            stage_sem.at[lax.rem(j, 2)],
        )

    for side in range(2):

        def grad(j, carry):
            columns = pl.ds(pl.multiple_of(j * width, width), width)
            total = jnp.dot(
                weight[side * 4], own[1 - side, :, columns], preferred_element_type=jnp.float32
            )
            for k in (1, 2, 3):
                total += jnp.dot(
                    weight[side * 4 + k],
                    far[side * 3 + k - 1, :, columns],
                    preferred_element_type=jnp.float32,
                )

            @pl.when(j >= 2)
            def _():
                out_copy(side, j - 2).wait()

            stage[lax.rem(j, 2)] = (total * factor).astype(jnp.bfloat16)
            out_copy(side, j).start()
            return carry

        lax.fori_loop(0, parts, grad, 0)
        out_copy(side, parts - 2).wait()
        out_copy(side, parts - 1).wait()

    over_pieces(lambda s: q_up(s).wait_send())
    over_pieces(lambda s: p_down(s).wait_send())
    over_pieces(lambda s: p_on(s).wait_send())
    over_pieces(lambda s: q_on(s).wait_send())

    @pl.when(second == 0)
    def _():
        over_pieces(lambda s: first_own(s).wait_send())
        over_pieces(lambda s: first_on(s).wait_send())

    @pl.when(second == 1)
    def _():
        over_pieces(lambda s: second_own(s).wait_send())
        over_pieces(lambda s: second_on(s).wait_send())


def local(n, queries, passages, links, positives):
    block, depth = queries.shape
    width = min(512, depth // 2)
    flops = 16 * 2 * block * block * depth
    query_grad, passage_grad, row_loss, col_loss = pl.pallas_call(
        functools.partial(kernel, n),
        out_shape=(
            jax.ShapeDtypeStruct((block, depth), jnp.bfloat16),
            jax.ShapeDtypeStruct((block, depth), jnp.bfloat16),
            jax.ShapeDtypeStruct((1, block), jnp.float32),
            jax.ShapeDtypeStruct((1, block), jnp.float32),
        ),
        in_specs=[
            pl.BlockSpec(memory_space=pl.ANY),
            pl.BlockSpec(memory_space=pl.ANY),
            pl.BlockSpec(memory_space=pltpu.SMEM),
            pl.BlockSpec(memory_space=pltpu.VMEM),
        ],
        out_specs=(
            pl.BlockSpec(memory_space=pl.ANY),
            pl.BlockSpec(memory_space=pl.ANY),
            pl.BlockSpec(memory_space=pltpu.VMEM),
            pl.BlockSpec(memory_space=pltpu.VMEM),
        ),
        scratch_shapes=[
            pltpu.VMEM((2, block, depth), jnp.bfloat16),
            pltpu.VMEM((6, block, depth), jnp.bfloat16),
            pltpu.VMEM((8, block, block), jnp.float32),
            pltpu.VMEM((8, block, block), jnp.bfloat16),
            pltpu.VMEM((2, block, 128), jnp.float32),
            pltpu.VMEM((2, block, width), jnp.bfloat16),
            pltpu.VMEM((2, block, block), jnp.float32),
            pltpu.VMEM((2, 8, block), jnp.float32),
            pltpu.VMEM((6, 8, block), jnp.float32),
            pltpu.VMEM((3, 8, 128), jnp.float32),
            pltpu.VMEM((3, 8, 128), jnp.float32),
            pltpu.SemaphoreType.DMA((2,)),
            pltpu.SemaphoreType.DMA((6, PIECES)),
            pltpu.SemaphoreType.DMA((6, PIECES)),
            pltpu.SemaphoreType.DMA((6,)),
            pltpu.SemaphoreType.DMA((6,)),
            pltpu.SemaphoreType.DMA((3,)),
            pltpu.SemaphoreType.DMA((3,)),
            pltpu.SemaphoreType.DMA((2,)),
        ],
        cost_estimate=pl.CostEstimate(
            flops=flops, bytes_accessed=8 * block * depth, transcendentals=24 * block * block
        ),
        compiler_params=pltpu.CompilerParams(
            collective_id=0, has_side_effects=True, vmem_limit_bytes=60 * 1024 * 1024
        ),
    )(queries, passages, links, positives)
    return query_grad, passage_grad, row_loss.reshape(block), col_loss.reshape(block)


def solution(mesh):
    placed = (P("dp", None), P("dp", None), P("dp", None), P("dp", None))
    return jax.shard_map(
        functools.partial(local, mesh.size),
        mesh=mesh,
        in_specs=placed,
        out_specs=(P("dp", None), P("dp", None), P("dp"), P("dp")),
        check_vma=False,
    )
```

time: 619 us -> 198 us (0.32)
  the two profiles are of different devices: /device:TPU:32 before, /device:TPU:1 now
where the time goes in v1:
time: 198 us
  Pallas kernels  189 us (95%)
  local copies, waits for them, and re-layouts  8.03 us (4%)
    pallas_call x1, Pallas kernels, local(): pl.pallas_call(functools.partial(kernel, n), out_shape=(jax.ShapeDtypeStr...  189 us
    unnamed x10, local copies, waits for them, and re-layouts  8.03 us

profile of v1, /device:TPU:1, one launch (start us, length us, event | category | flops | bytes accessed | tf_op | source)
XLA Modules:
  0.0 198.0 jit_solution(8401242904216844906)
XLA Ops:
  0.6 189.3 %shard_map.75 = (bf16[512,4096]{1,0:T(8,128)(2,1)}, bf16[512,4096]{1,0:T(8,128)(2,1)}, f32[1,512]{1,0:T(1,128)}, f32[1,512]{1,0:T(1,128)}) custom-call(bf16[512,4096]{1,0:T(8,128)(2,1)} %q_hbm.1, bf16[512,4096]{1,0:T(8,128)(2,1)} %p_hbm.1, s32[1,3]{1,0:T(1,128)} %links_ref.1, s32[1,512]{1,0:T(1,128)} %pos_ref.1), custom_call_target="tpu_custom_call" | custom-call | flops 34359738368 | bytes 16777216 | tf_op jit(solution)/shard_map/pallas_call | solution.py:326
  190.0 0.0 copy-start
  190.0 4.8 %copy.12 = bf16[512,4096]{1,0:T(8,128)(2,1)} copy(bf16[512,4096]{1,0:T(8,128)(2,1)} %get-tuple-element.16) | data formatting | bytes 8388608
  194.8 0.0 copy-done
  194.8 0.0 copy-start.2
  194.8 0.0 copy-start.1
  194.8 2.0 %copy.13 = bf16[512,4096]{1,0:T(8,128)(2,1)} copy(bf16[512,4096]{1,0:T(8,128)(2,1)S(1)} %copy-done) | data formatting | bytes 8388608
  196.8 0.0 copy-done.2
  196.8 0.6 copy.14
  197.4 0.0 copy-done.1
  197.4 0.6 copy.15
Async XLA Ops:
  190.0 4.9 %copy-start = (bf16[512,4096]{1,0:T(8,128)(2,1)S(1)}, bf16[512,4096]{1,0:T(8,128)(2,1)}, u32[]{:S(2)}) copy-start(bf16[512,4096]{1,0:T(8,128)(2,1)} %get-tuple-element.17) | copy-start | bytes 12582916
  194.8 2.0 %copy-start.2 = (f32[1,512]{1,0:T(1,128)S(1)}, f32[1,512]{1,0:T(1,128)}, u32[]{:S(2)}) copy-start(f32[1,512]{1,0:T(1,128)} %get-tuple-element.10) | copy-start | bytes 6148
  194.8 2.6 %copy-start.1 = (f32[1,512]{1,0:T(1,128)S(1)}, f32[1,512]{1,0:T(1,128)}, u32[]{:S(2)}) copy-start(f32[1,512]{1,0:T(1,128)} %get-tuple-element.11) | copy-start | bytes 6148

commit v2 on v1

v2 whole, which is shorter than its diff:
```python
import functools

import jax
import jax.numpy as jnp
from jax import lax
from jax.experimental import pallas as pl
from jax.experimental.pallas import tpu as pltpu
from jax.sharding import PartitionSpec as P

MESH = pl.DeviceIdType.MESH
NEG = -1e30
PIECES = 4
STRIP = 64


def kernel(
    n,
    q_hbm,
    p_hbm,
    links_ref,
    pos_ref,
    dq_hbm,
    dp_hbm,
    row_ref,
    col_ref,
    own,
    far,
    acc,
    weight,
    top,
    mass,
    lse,
    stage,
    upright,
    hit,
    said,
    heard,
    extra,
    stat_out,
    stat_in,
    flag_out,
    flag_in,
    load_sem,
    send_sem,
    recv_sem,
    said_sem,
    heard_sem,
    flag_send_sem,
    flag_recv_sem,
    stat_send_sem,
    stat_recv_sem,
    stage_sem,
):
    block, depth = q_hbm.shape
    factor = depth ** (-0.5)
    rows = block // PIECES
    me = lax.axis_index("dp")
    second = lax.rem(me, 2)
    is_first = second == 0
    is_second = second == 1
    late = (2, 4 + second)

    def at(offset):
        return (lax.rem(me + offset + n, n),)

    barrier = pltpu.get_barrier_semaphore()
    for offset in (1, 2, 3, 4, -1, -2, -3, -4):
        pl.semaphore_signal(barrier, inc=1, device_id=at(offset), device_id_type=MESH)
    pl.semaphore_wait(barrier, 8)

    def piece(s):
        return pl.ds(pl.multiple_of(s * rows, rows), rows)

    def send(stream, s, src, slot, offset):
        return pltpu.make_async_remote_copy(
            src_ref=src.at[piece(s)],
            dst_ref=far.at[slot, piece(s)],
            send_sem=send_sem.at[stream, s],
            recv_sem=recv_sem.at[slot, s],
            device_id=at(offset),
            device_id_type=MESH,
        )

    def q_up(s):
        return send(0, s, q_hbm, 4, 2)

    def p_down(s):
        return send(1, s, p_hbm, 1, -2)

    def p_on(s):
        return send(2, s, far.at[1], 2, -1)

    def q_on(s):
        return send(3, s, far.at[4], 5, 1)

    def first_own(s):
        return send(4, s, q_hbm, 3, 1)

    def first_on(s):
        return send(5, s, far.at[1], 0, 1)

    def second_own(s):
        return send(4, s, p_hbm, 0, -1)

    def second_on(s):
        return send(5, s, far.at[4], 3, -1)

    def q_pass(s):
        return send(7, s, far.at[3], 4, 1)

    def p_pass(s):
        return send(6, s, far.at[0], 2, -2)

    def arrived(slot, s):
        send(0, s, q_hbm, slot, 1).wait_recv()

    def loop(count, body):
        def step(s, carry):
            body(s)
            return carry

        lax.fori_loop(0, count, step, 0)

    for k in range(3):
        flag_out[k] = jnp.full((8, 128), links_ref[0, k].astype(jnp.float32), jnp.float32)

    def flag_copy(k):
        return pltpu.make_async_remote_copy(
            src_ref=flag_out.at[k],
            dst_ref=flag_in.at[k],
            send_sem=flag_send_sem.at[k],
            recv_sem=flag_recv_sem.at[k],
            device_id=at(k + 1),
            device_id_type=MESH,
        )

    for k in range(3):
        flag_copy(k).start()

    @pl.when(is_first)
    def _():
        loop(PIECES, lambda s: p_down(s).start())
        loop(PIECES, lambda s: first_own(s).start())

    @pl.when(is_second)
    def _():
        loop(PIECES, lambda s: q_up(s).start())
        loop(PIECES, lambda s: p_down(s).start())
        loop(PIECES, lambda s: second_own(s).start())

    load_q = pltpu.make_async_copy(q_hbm, own.at[0], load_sem.at[0])
    load_p = pltpu.make_async_copy(p_hbm, own.at[1], load_sem.at[1])
    load_q.start()
    load_p.start()

    pos = pos_ref[...].astype(jnp.float32)
    upright[...] = jnp.transpose(jnp.broadcast_to(pos, (128, block)))
    top[...] = jnp.full(top.shape, NEG, jnp.float32)
    mass[...] = jnp.zeros(mass.shape, jnp.float32)

    @pl.when(is_first)
    def _():
        line = lax.broadcasted_iota(jnp.int32, (8, block), 0)
        stat_in[0] = jnp.where(line < 4, NEG, 0.0)

    load_q.wait()
    load_p.wait()

    def dot_t(a, b):
        return lax.dot_general(a, b, (((1,), (1,)), ((), ())), preferred_element_type=jnp.float32)

    def fold(side, part):
        before = top[side]
        now = jnp.maximum(before, part)
        mass[side] = mass[side] * jnp.exp(before - now) + jnp.exp(part - now)
        top[side] = now

    def diagonal(t):
        side, s = t // PIECES, lax.rem(t, PIECES)
        part = dot_t(own[side], own[1 - side, piece(s), :]) * factor
        acc[0, side * 3, :, piece(s)] = part
        fold(side, part)

    loop(2 * PIECES, diagonal)
    down = lax.broadcasted_iota(jnp.int32, (block, block), 0).astype(jnp.float32)
    across = lax.broadcasted_iota(jnp.int32, (block, block), 1).astype(jnp.float32)
    row_hit = jnp.sum(jnp.where(pos == down, acc[0, 3], 0.0), axis=0, keepdims=True)
    hit[0] = jnp.broadcast_to(row_hit, (8, block))
    col_hit = jnp.sum(
        jnp.where(upright[:, 0:1] == across, acc[0, 0], 0.0), axis=0, keepdims=True
    )
    hit[1] = jnp.broadcast_to(col_hit, (8, block))
    for k in range(3):
        flag_copy(k).wait_recv()

    def live(side, part, k):
        flag = (flag_out if side == 0 else flag_in)[k - 1, 0:1, 0:1]
        return jnp.where(flag > 0, part, NEG)

    def scores(side, slot, k, s):
        return live(side, dot_t(own[side], far[slot, piece(s), :]) * factor, k)

    def tell_stats(index, part, s):
        largest = jnp.max(part, axis=0, keepdims=True)
        total = jnp.sum(jnp.exp(part - largest), axis=0, keepdims=True)
        line = lax.broadcasted_iota(jnp.int32, (8, rows), 0)
        stat_out[index, :, piece(s)] = jnp.where(line < 4, largest, total)

    def first_far(s):
        arrived(5, s)
        part = scores(1, 5, 3, s)
        acc[0, 5, :, piece(s)] = part
        fold(1, part)
        tell_stats(2, part, s)

    def near(s):
        arrived(1, s)

        @pl.when(is_first)
        def _():
            first_on(s).start()

        @pl.when(is_second)
        def _():
            p_on(s).start()

        part = scores(0, 1, 2, s)
        acc[0, 2, :, piece(s)] = part
        fold(0, part)

        @pl.when(is_first)
        def _():
            tell_stats(0, part, s)

        @pl.when(is_first)
        def _():
            arrived(3, s)

        part = scores(1, 3, 1, s)
        acc[0, 4, :, piece(s)] = part
        fold(1, part)
        arrived(0, s)

        @pl.when(is_second)
        def _():
            p_pass(s).start()

        part = scores(0, 0, 1, s)
        acc[0, 1, :, piece(s)] = part
        fold(0, part)

        @pl.when(is_first)
        def _():
            arrived(2, s)
            part = scores(0, 2, 3, s)
            fold(0, part)
            tell_stats(1, part, s)

            @pl.when(s >= 1)
            def _():
                first_far(s - 1)

    @pl.when(is_second)
    def _():
        loop(PIECES, lambda s: arrived(3, s))

        def early(u):
            arrived(4, u)
            q_on(u).start()
            second_on(u).start()
            part = scores(1, 4, 2, u)
            acc[0, 5, :, piece(u)] = part
            fold(1, part)

        loop(PIECES, early)
        loop(PIECES, lambda u: q_pass(u).start())

    loop(PIECES, near)

    def stat_copy(index, slot, offset):
        return pltpu.make_async_remote_copy(
            src_ref=stat_out.at[index],
            dst_ref=stat_in.at[slot],
            send_sem=stat_send_sem.at[index],
            recv_sem=stat_recv_sem.at[slot],
            device_id=at(offset),
            device_id_type=MESH,
        )

    stat_copies = (stat_copy(0, 1, 2), stat_copy(1, 1, 3), stat_copy(2, 0, -3))

    @pl.when(is_first)
    def _():
        stat_copies[0].start()
        stat_copies[1].start()
        first_far(PIECES - 1)
        stat_copies[2].start()

    @pl.when(is_second)
    def _():
        stat_copies[2].wait_recv()

    stat_copies[0].wait_recv()

    def tell(index, src, dst, offset):
        return pltpu.make_async_remote_copy(
            src_ref=src,
            dst_ref=extra if dst is None else heard.at[dst],
            send_sem=said_sem.at[index],
            recv_sem=heard_sem.at[6 if dst is None else dst],
            device_id=at(offset),
            device_id_type=MESH,
        )

    def first_tells(side):
        sign = 1 if side == 0 else -1
        return [
            tell(side * 3 + k - 1, said.at[side], (1 - side) * 3 + k - 1, sign * k)
            for k in (1, 2, 3)
        ]

    def passed_tells():
        up = [tell(6 + k, extra, 3 + k, 2 + k) for k in range(3)]
        return up + [tell(8 + k, heard.at[0], k, -k) for k in (1, 2)]

    def second_tells(side):
        return [tell(side, said.at[side], None if side == 0 else 0, -1)]

    for side in range(2):
        tops = jnp.transpose(top[side])
        largest = jnp.max(tops, axis=0, keepdims=True)
        total = jnp.sum(
            jnp.transpose(mass[side]) * jnp.exp(tops - largest), axis=0, keepdims=True
        )
        other = stat_in[side, 0:1, :]
        both = jnp.maximum(largest, other)
        total = total * jnp.exp(largest - both) + stat_in[side, 4:5, :] * jnp.exp(other - both)
        value = both + jnp.log(total)
        said[side] = jnp.broadcast_to(value, (8, block))

        @pl.when(is_first)
        def _():
            for copy in first_tells(side):
                copy.start()

        @pl.when(is_second)
        def _():
            for copy in second_tells(side):
                copy.start()

        lse[side] = jnp.transpose(jnp.broadcast_to(value, (128, block)))

    row_ref[...] = said[0, 0:1, :] - hit[0, 0:1, :]
    col_ref[...] = said[1, 0:1, :] - hit[1, 0:1, :]

    strips = block // STRIP

    def strip(i):
        return pl.ds(pl.multiple_of(i * STRIP, STRIP), STRIP)

    def weigh(side, index, theirs, i):
        tile = acc[0, side * 3 + index, strip(i), :]
        value = jnp.exp(tile - lse[side, strip(i), 0:1]) + jnp.exp(tile - theirs)
        if index == 0:
            if side == 0:
                lanes = lax.broadcasted_iota(jnp.int32, (STRIP, block), 1).astype(jnp.float32)
                match = upright[strip(i), 0:1] == lanes
            else:
                lines = lax.broadcasted_iota(jnp.int32, (STRIP, block), 0) + i * STRIP
                match = pos_ref[...] == lines
            value = value - jnp.where(match, 2.0, 0.0)
        weight[side * 3 + index, strip(i), :] = value.astype(jnp.bfloat16)

    def weigh_diagonal(i):
        for side in range(2):
            weigh(side, 0, said[1 - side, 0:1, :], i)

    def told(dst):
        tell(0, said.at[0], dst, 1).wait_recv()

    told(0)

    @pl.when(is_first)
    def _():
        told(None)
        for copy in passed_tells():
            copy.start()

    loop(strips, weigh_diagonal)
    for dst in range(1, 6):
        told(dst)

    def weigh_far(i):
        weigh(0, 1, heard[0, 0:1, :], i)
        weigh(0, 2, heard[1, 0:1, :], i)
        weigh(1, 1, heard[3, 0:1, :], i)
        weigh(1, 2, heard[5 - second, 0:1, :], i)

    loop(strips, weigh_far)

    width = stage.shape[2]
    parts = depth // width

    def columns(j):
        return pl.ds(pl.multiple_of(j * width, width), width)

    for side in range(2):

        def early_grad(j):
            slots = (0, 1) if side == 0 else (3, 5 - second)
            total = jnp.dot(
                weight[side * 3], own[1 - side, :, columns(j)], preferred_element_type=jnp.float32
            )
            for index, slot in enumerate(slots):
                total += jnp.dot(
                    weight[side * 3 + 1 + index],
                    far[slot, :, columns(j)],
                    preferred_element_type=jnp.float32,
                )
            acc[side, j] = total

        loop(parts, early_grad)

    def weigh_late(side, s):
        slot = late[side]
        k = 3 if side == 0 else 2 + second
        part = scores(side, slot, k, s)
        theirs = heard[slot, 0:1, piece(s)]
        value = jnp.exp(part - lse[side, :, 0:1]) + jnp.exp(part - theirs)
        weight[6 + side, :, piece(s)] = value.astype(jnp.bfloat16)

    def out_copy(side, j):
        hbm = dq_hbm if side == 0 else dp_hbm
        return pltpu.make_async_copy(
            stage.at[lax.rem(j, 2)], hbm.at[:, columns(j)], stage_sem.at[lax.rem(j, 2)]
        )

    def finish(side):
        def late_grad(j):
            total = acc[side, j] + jnp.dot(
                weight[6 + side], far[late[side], :, columns(j)], preferred_element_type=jnp.float32
            )

            @pl.when(j >= 2)
            def _():
                out_copy(side, j - 2).wait()

            stage[lax.rem(j, 2)] = (total * factor).astype(jnp.bfloat16)
            out_copy(side, j).start()

        loop(parts, late_grad)
        out_copy(side, parts - 2).wait()
        out_copy(side, parts - 1).wait()

    def late_piece(s):
        @pl.when(is_second)
        def _():
            arrived(2, s)

        weigh_late(0, s)

        @pl.when(is_first)
        def _():
            arrived(4, s)
            q_on(s).start()

        @pl.when(is_second)
        def _():
            arrived(5, s)

        weigh_late(1, s)

    loop(PIECES, late_piece)
    finish(0)
    finish(1)

    for k in range(3):
        flag_copy(k).wait_send()
    for copy in (p_down, q_on):
        loop(PIECES, lambda s: copy(s).wait_send())

    @pl.when(is_first)
    def _():
        for copy in (first_own, first_on):
            loop(PIECES, lambda s: copy(s).wait_send())
        for copy in stat_copies + tuple(first_tells(0) + first_tells(1) + passed_tells()):
            copy.wait_send()

    @pl.when(is_second)
    def _():
        for copy in (q_up, p_on, second_own, second_on, p_pass, q_pass):
            loop(PIECES, lambda s: copy(s).wait_send())
        for copy in second_tells(0) + second_tells(1):
            copy.wait_send()


def local(n, queries, passages, links, positives):
    block, depth = queries.shape
    width = min(block, depth // 2)
    flops = 16 * 2 * block * block * depth
    query_grad, passage_grad, row_loss, col_loss = pl.pallas_call(
        functools.partial(kernel, n),
        out_shape=(
            jax.ShapeDtypeStruct((block, depth), jnp.bfloat16),
            jax.ShapeDtypeStruct((block, depth), jnp.bfloat16),
            jax.ShapeDtypeStruct((1, block), jnp.float32),
            jax.ShapeDtypeStruct((1, block), jnp.float32),
        ),
        in_specs=[
            pl.BlockSpec(memory_space=pl.ANY),
            pl.BlockSpec(memory_space=pl.ANY),
            pl.BlockSpec(memory_space=pltpu.SMEM),
            pl.BlockSpec(memory_space=pltpu.VMEM),
        ],
        out_specs=(
            pl.BlockSpec(memory_space=pl.ANY),
            pl.BlockSpec(memory_space=pl.ANY),
            pl.BlockSpec(memory_space=pltpu.VMEM),
            pl.BlockSpec(memory_space=pltpu.VMEM),
        ),
        scratch_shapes=[
            pltpu.VMEM((2, block, depth), jnp.bfloat16),
            pltpu.VMEM((6, block, depth), jnp.bfloat16),
            pltpu.VMEM((2, max(depth // width, 6), block, width), jnp.float32),
            pltpu.VMEM((8, block, block), jnp.bfloat16),
            pltpu.VMEM((2, block, 128), jnp.float32),
            pltpu.VMEM((2, block, 128), jnp.float32),
            pltpu.VMEM((2, block, 128), jnp.float32),
            pltpu.VMEM((2, block, width), jnp.bfloat16),
            pltpu.VMEM((block, 128), jnp.float32),
            pltpu.VMEM((2, 8, block), jnp.float32),
            pltpu.VMEM((2, 8, block), jnp.float32),
            pltpu.VMEM((6, 8, block), jnp.float32),
            pltpu.VMEM((8, block), jnp.float32),
            pltpu.VMEM((3, 8, block), jnp.float32),
            pltpu.VMEM((2, 8, block), jnp.float32),
            pltpu.VMEM((3, 8, 128), jnp.float32),
            pltpu.VMEM((3, 8, 128), jnp.float32),
            pltpu.SemaphoreType.DMA((2,)),
            pltpu.SemaphoreType.DMA((8, PIECES)),
            pltpu.SemaphoreType.DMA((6, PIECES)),
            pltpu.SemaphoreType.DMA((11,)),
            pltpu.SemaphoreType.DMA((7,)),
            pltpu.SemaphoreType.DMA((3,)),
            pltpu.SemaphoreType.DMA((3,)),
            pltpu.SemaphoreType.DMA((3,)),
            pltpu.SemaphoreType.DMA((2,)),
            pltpu.SemaphoreType.DMA((2,)),
        ],
        cost_estimate=pl.CostEstimate(
            flops=flops, bytes_accessed=8 * block * depth, transcendentals=24 * block * block
        ),
        compiler_params=pltpu.CompilerParams(
            collective_id=0, has_side_effects=True, vmem_limit_bytes=60 * 1024 * 1024
        ),
    )(queries, passages, links, positives)
    return query_grad, passage_grad, row_loss.reshape(block), col_loss.reshape(block)


def solution(mesh):
    placed = (P("dp", None), P("dp", None), P("dp", None), P("dp", None))
    return jax.shard_map(
        functools.partial(local, mesh.size),
        mesh=mesh,
        in_specs=placed,
        out_specs=(P("dp", None), P("dp", None), P("dp"), P("dp")),
        check_vma=False,
    )
```

time: 198 us -> 184 us (0.929)
  Pallas kernels: 189 us -> 175 us
    pallas_call x1, Pallas kernels: 189 us -> 175 us  [local(): pl.pallas_call(functools.partial(kernel, n), out_shape=(jax.ShapeDtypeStr...]
where the time goes in v2:
time: 184 us
  Pallas kernels  175 us (95%)
  local copies, waits for them, and re-layouts  8.03 us (4%)
    pallas_call x1, Pallas kernels, local(): pl.pallas_call(functools.partial(kernel, n), out_shape=(jax.ShapeDtypeStr...  175 us
    unnamed x10, local copies, waits for them, and re-layouts  8.03 us

profile of v2, /device:TPU:1, one launch (start us, length us, event | category | flops | bytes accessed | tf_op | source)
XLA Modules:
  0.0 183.9 jit_solution(7885391908162111697)
XLA Ops:
  0.6 175.2 %shard_map.75 = (bf16[512,4096]{1,0:T(8,128)(2,1)}, bf16[512,4096]{1,0:T(8,128)(2,1)}, f32[1,512]{1,0:T(1,128)}, f32[1,512]{1,0:T(1,128)}) custom-call(bf16[512,4096]{1,0:T(8,128)(2,1)} %q_hbm.1, bf16[512,4096]{1,0:T(8,128)(2,1)} %p_hbm.1, s32[1,3]{1,0:T(1,128)} %links_ref.1, s32[1,512]{1,0:T(1,128)} %pos_ref.1), custom_call_target="tpu_custom_call" | custom-call | flops 34359738368 | bytes 16777216 | tf_op jit(solution)/shard_map/pallas_call | solution.py:501
  175.9 0.0 copy-start
  175.9 4.8 %copy.12 = bf16[512,4096]{1,0:T(8,128)(2,1)} copy(bf16[512,4096]{1,0:T(8,128)(2,1)} %get-tuple-element.16) | data formatting | bytes 8388608
  180.7 0.0 copy-done
  180.7 0.0 copy-start.2
  180.7 0.0 copy-start.1
  180.7 2.0 %copy.13 = bf16[512,4096]{1,0:T(8,128)(2,1)} copy(bf16[512,4096]{1,0:T(8,128)(2,1)S(1)} %copy-done) | data formatting | bytes 8388608
  182.8 0.0 copy-done.2
  182.8 0.6 copy.14
  183.3 0.0 copy-done.1
  183.3 0.6 copy.15
Async XLA Ops:
  175.9 4.9 %copy-start = (bf16[512,4096]{1,0:T(8,128)(2,1)S(1)}, bf16[512,4096]{1,0:T(8,128)(2,1)}, u32[]{:S(2)}) copy-start(bf16[512,4096]{1,0:T(8,128)(2,1)} %get-tuple-element.17) | copy-start | bytes 12582916
  180.7 2.0 %copy-start.2 = (f32[1,512]{1,0:T(1,128)S(1)}, f32[1,512]{1,0:T(1,128)}, u32[]{:S(2)}) copy-start(f32[1,512]{1,0:T(1,128)} %get-tuple-element.10) | copy-start | bytes 6148
  180.7 2.6 %copy-start.1 = (f32[1,512]{1,0:T(1,128)S(1)}, f32[1,512]{1,0:T(1,128)}, u32[]{:S(2)}) copy-start(f32[1,512]{1,0:T(1,128)} %get-tuple-element.11) | copy-start | bytes 6148

commit v3 on v2

--- a/solution.py
+++ b/solution.py
@@ -175,19 +175,26 @@
         mass[side] = mass[side] * jnp.exp(before - now) + jnp.exp(part - now)
         top[side] = now
 
+    def tile(index, start, size):
+        per = stage.shape[2] // block
+        first = lax.rem(index, per) * block + start
+        return (0, index // per, slice(None), pl.ds(pl.multiple_of(first, 128), size))
+
+    def keep(side, index, part, s):
+        acc[tile(index, s * rows, rows)] = part
+        fold(side, part)
+
     def diagonal(t):
         side, s = t // PIECES, lax.rem(t, PIECES)
-        part = dot_t(own[side], own[1 - side, piece(s), :]) * factor
-        acc[0, side * 3, :, piece(s)] = part
-        fold(side, part)
+        keep(side, side * 3, dot_t(own[side], own[1 - side, piece(s), :]) * factor, s)
 
     loop(2 * PIECES, diagonal)
     down = lax.broadcasted_iota(jnp.int32, (block, block), 0).astype(jnp.float32)
     across = lax.broadcasted_iota(jnp.int32, (block, block), 1).astype(jnp.float32)
-    row_hit = jnp.sum(jnp.where(pos == down, acc[0, 3], 0.0), axis=0, keepdims=True)
+    row_hit = jnp.sum(jnp.where(pos == down, acc[tile(3, 0, block)], 0.0), axis=0, keepdims=True)
     hit[0] = jnp.broadcast_to(row_hit, (8, block))
     col_hit = jnp.sum(
-        jnp.where(upright[:, 0:1] == across, acc[0, 0], 0.0), axis=0, keepdims=True
+        jnp.where(upright[:, 0:1] == across, acc[tile(0, 0, block)], 0.0), axis=0, keepdims=True
     )
     hit[1] = jnp.broadcast_to(col_hit, (8, block))
     for k in range(3):
@@ -197,85 +204,20 @@
         flag = (flag_out if side == 0 else flag_in)[k - 1, 0:1, 0:1]
         return jnp.where(flag > 0, part, NEG)
 
-    def scores(side, slot, k, s):
-        return live(side, dot_t(own[side], far[slot, piece(s), :]) * factor, k)
+    def scores(side, slot, k, start, size):
+        lines = pl.ds(pl.multiple_of(start, 128), size)
+        return live(side, dot_t(own[side], far[slot, lines, :]) * factor, k)
+
+    def score_piece(side, slot, k, index, s):
+        part = scores(side, slot, k, s * rows, rows)
+        keep(side, index, part, s)
+        return part
 
     def tell_stats(index, part, s):
         largest = jnp.max(part, axis=0, keepdims=True)
         total = jnp.sum(jnp.exp(part - largest), axis=0, keepdims=True)
         line = lax.broadcasted_iota(jnp.int32, (8, rows), 0)
         stat_out[index, :, piece(s)] = jnp.where(line < 4, largest, total)
-
-    def first_far(s):
-        arrived(5, s)
-        part = scores(1, 5, 3, s)
-        acc[0, 5, :, piece(s)] = part
-        fold(1, part)
-        tell_stats(2, part, s)
-
-    def near(s):
-        arrived(1, s)
-
-        @pl.when(is_first)
-        def _():
-            first_on(s).start()
-
-        @pl.when(is_second)
-        def _():
-            p_on(s).start()
-
-        part = scores(0, 1, 2, s)
-        acc[0, 2, :, piece(s)] = part
-        fold(0, part)
-
-        @pl.when(is_first)
-        def _():
-            tell_stats(0, part, s)
-
-        @pl.when(is_first)
-        def _():
-            arrived(3, s)
-
-        part = scores(1, 3, 1, s)
-        acc[0, 4, :, piece(s)] = part
-        fold(1, part)
-        arrived(0, s)
-
-        @pl.when(is_second)
-        def _():
-            p_pass(s).start()
-
-        part = scores(0, 0, 1, s)
-        acc[0, 1, :, piece(s)] = part
-        fold(0, part)
-
-        @pl.when(is_first)
-        def _():
-            arrived(2, s)
-            part = scores(0, 2, 3, s)
-            fold(0, part)
-            tell_stats(1, part, s)
-
-            @pl.when(s >= 1)
-            def _():
-                first_far(s - 1)
-
-    @pl.when(is_second)
-    def _():
-        loop(PIECES, lambda s: arrived(3, s))
-
-        def early(u):
-            arrived(4, u)
-            q_on(u).start()
-            second_on(u).start()
-            part = scores(1, 4, 2, u)
-            acc[0, 5, :, piece(u)] = part
-            fold(1, part)
-
-        loop(PIECES, early)
-        loop(PIECES, lambda u: q_pass(u).start())
-
-    loop(PIECES, near)
 
     def stat_copy(index, slot, offset):
         return pltpu.make_async_remote_copy(
@@ -291,9 +233,70 @@
 
     @pl.when(is_first)
     def _():
-        stat_copies[0].start()
-        stat_copies[1].start()
-        first_far(PIECES - 1)
+        def early(s):
+            arrived(0, s)
+            score_piece(0, 0, 1, 1, s)
+
+        def soon(s):
+            arrived(3, s)
+            score_piece(1, 3, 1, 4, s)
+
+        loop(PIECES, early)
+        loop(PIECES, soon)
+
+    @pl.when(is_second)
+    def _():
+        def early(s):
+            arrived(3, s)
+            score_piece(1, 3, 1, 4, s)
+
+        def soon(s):
+            arrived(4, s)
+            q_on(s).start()
+            second_on(s).start()
+            score_piece(1, 4, 2, 5, s)
+
+        loop(PIECES, early)
+        loop(PIECES, soon)
+        loop(PIECES, lambda s: q_pass(s).start())
+
+    def near(s):
+        arrived(1, s)
+
+        @pl.when(is_first)
+        def _():
+            first_on(s).start()
+
+        @pl.when(is_second)
+        def _():
+            p_on(s).start()
+
+        part = score_piece(0, 1, 2, 2, s)
+
+        @pl.when(is_first)
+        def _():
+            tell_stats(0, part, s)
+            arrived(2, s)
+            tell_stats(1, score_piece(0, 2, 3, 6, s), s)
+
+            @pl.when(s == PIECES - 1)
+            def _():
+                stat_copies[0].start()
+                stat_copies[1].start()
+
+            arrived(5, s)
+            tell_stats(2, score_piece(1, 5, 3, 5, s), s)
+
+        @pl.when(is_second)
+        def _():
+            arrived(0, s)
+            p_pass(s).start()
+            score_piece(0, 0, 1, 1, s)
+
+    loop(PIECES, near)
+
+    @pl.when(is_first)
+    def _():
         stat_copies[2].start()
 
     @pl.when(is_second)
@@ -359,17 +362,20 @@
         return pl.ds(pl.multiple_of(i * STRIP, STRIP), STRIP)
 
     def weigh(side, index, theirs, i):
-        tile = acc[0, side * 3 + index, strip(i), :]
-        value = jnp.exp(tile - lse[side, strip(i), 0:1]) + jnp.exp(tile - theirs)
+        per = stage.shape[2] // block
+        at_tile = side * 3 + index if index < 3 else 6
+        lanes = pl.ds(at_tile % per * block, block)
+        score = acc[0, at_tile // per, strip(i), lanes]
+        value = jnp.exp(score - lse[side, strip(i), 0:1]) + jnp.exp(score - theirs)
         if index == 0:
             if side == 0:
-                lanes = lax.broadcasted_iota(jnp.int32, (STRIP, block), 1).astype(jnp.float32)
-                match = upright[strip(i), 0:1] == lanes
+                across = lax.broadcasted_iota(jnp.int32, (STRIP, block), 1)
+                match = upright[strip(i), 0:1] == across.astype(jnp.float32)
             else:
                 lines = lax.broadcasted_iota(jnp.int32, (STRIP, block), 0) + i * STRIP
                 match = pos_ref[...] == lines
             value = value - jnp.where(match, 2.0, 0.0)
-        weight[side * 3 + index, strip(i), :] = value.astype(jnp.bfloat16)
+        weight[at_tile, strip(i), :] = value.astype(jnp.bfloat16)
 
     def weigh_diagonal(i):
         for side in range(2):
@@ -398,14 +404,17 @@
 
     loop(strips, weigh_far)
 
+    @pl.when(is_first)
+    def _():
+        loop(strips, lambda i: weigh(0, 3, heard[2, 0:1, :], i))
+
     width = stage.shape[2]
     parts = depth // width
 
     def columns(j):
         return pl.ds(pl.multiple_of(j * width, width), width)
 
-    for side in range(2):
-
+    def early_grads(side):
         def early_grad(j):
             slots = (0, 1) if side == 0 else (3, 5 - second)
             total = jnp.dot(
@@ -421,13 +430,13 @@
 
         loop(parts, early_grad)
 
-    def weigh_late(side, s):
+    def weigh_late(side, start, size):
         slot = late[side]
         k = 3 if side == 0 else 2 + second
-        part = scores(side, slot, k, s)
-        theirs = heard[slot, 0:1, piece(s)]
+        part = scores(side, slot, k, start, size)
+        theirs = heard[slot, 0:1, pl.ds(start, size)]
         value = jnp.exp(part - lse[side, :, 0:1]) + jnp.exp(part - theirs)
-        weight[6 + side, :, piece(s)] = value.astype(jnp.bfloat16)
+        weight[6 + side, :, pl.ds(start, size)] = value.astype(jnp.bfloat16)
 
     def out_copy(side, j):
         hbm = dq_hbm if side == 0 else dp_hbm
@@ -452,26 +461,41 @@
         out_copy(side, parts - 2).wait()
         out_copy(side, parts - 1).wait()
 
-    def late_piece(s):
-        @pl.when(is_second)
-        def _():
-            arrived(2, s)
-
-        weigh_late(0, s)
-
+    def forward(s):
         @pl.when(is_first)
         def _():
             arrived(4, s)
             q_on(s).start()
 
+    forward(0)
+    early_grads(1)
+    forward(1)
+    early_grads(0)
+    forward(2)
+
+    @pl.when(is_first)
+    def _():
+        finish(0)
+
+    for first, count in ((0, PIECES // 2), (PIECES // 2, 1), (PIECES // 2 + 1, 1)):
+        here = range(first, first + count)
+        if here[-1] == PIECES - 1:
+            forward(PIECES - 1)
+
         @pl.when(is_second)
         def _():
-            arrived(5, s)
-
-        weigh_late(1, s)
-
-    loop(PIECES, late_piece)
-    finish(0)
+            for s in here:
+                arrived(2, s)
+            weigh_late(0, first * rows, count * rows)
+            for s in here:
+                arrived(5, s)
+
+        weigh_late(1, first * rows, count * rows)
+
+    @pl.when(is_second)
+    def _():
+        finish(0)
+
     finish(1)
 
     for k in range(3):
@@ -496,7 +520,7 @@
 
 def local(n, queries, passages, links, positives):
     block, depth = queries.shape
-    width = min(block, depth // 2)
+    width = min(2 * block, depth // 2)
     flops = 16 * 2 * block * block * depth
     query_grad, passage_grad, row_loss, col_loss = pl.pallas_call(
         functools.partial(kernel, n),
@@ -521,7 +545,7 @@
         scratch_shapes=[
             pltpu.VMEM((2, block, depth), jnp.bfloat16),
             pltpu.VMEM((6, block, depth), jnp.bfloat16),
-            pltpu.VMEM((2, max(depth // width, 6), block, width), jnp.float32),
+            pltpu.VMEM((2, max(depth // width, -(-7 * block // width)), block, width), jnp.float32),
             pltpu.VMEM((8, block, block), jnp.bfloat16),
             pltpu.VMEM((2, block, 128), jnp.float32),
             pltpu.VMEM((2, block, 128), jnp.float32),

time: 184 us -> 172 us (0.935)
  Pallas kernels: 175 us -> 163 us
    pallas_call x1, Pallas kernels: 175 us -> 163 us  [local(): pl.pallas_call(functools.partial(kernel, n), out_shape=(jax.ShapeDtypeStr...]
where the time goes in v3:
time: 172 us
  Pallas kernels  163 us (95%)
  local copies, waits for them, and re-layouts  8.03 us (5%)
    pallas_call x1, Pallas kernels, local(): pl.pallas_call(functools.partial(kernel, n), out_shape=(jax.ShapeDtypeStr...  163 us
    unnamed x10, local copies, waits for them, and re-layouts  8.03 us

profile of v3, /device:TPU:1, one launch (start us, length us, event | category | flops | bytes accessed | tf_op | source)
XLA Modules:
  0.0 171.6 jit_solution(5259933519931090029)
XLA Ops:
  0.6 162.9 %shard_map.75 = (bf16[512,4096]{1,0:T(8,128)(2,1)}, bf16[512,4096]{1,0:T(8,128)(2,1)}, f32[1,512]{1,0:T(1,128)}, f32[1,512]{1,0:T(1,128)}) custom-call(bf16[512,4096]{1,0:T(8,128)(2,1)} %q_hbm.1, bf16[512,4096]{1,0:T(8,128)(2,1)} %p_hbm.1, s32[1,3]{1,0:T(1,128)} %links_ref.1, s32[1,512]{1,0:T(1,128)} %pos_ref.1), custom_call_target="tpu_custom_call" | custom-call | flops 34359738368 | bytes 16777216 | tf_op jit(solution)/shard_map/pallas_call | solution.py:525
  163.5 0.0 copy-start
  163.5 4.8 %copy.12 = bf16[512,4096]{1,0:T(8,128)(2,1)} copy(bf16[512,4096]{1,0:T(8,128)(2,1)} %get-tuple-element.16) | data formatting | bytes 8388608
  168.4 0.0 copy-done
  168.4 0.0 copy-start.2
  168.4 0.0 copy-start.1
  168.4 2.0 %copy.13 = bf16[512,4096]{1,0:T(8,128)(2,1)} copy(bf16[512,4096]{1,0:T(8,128)(2,1)S(1)} %copy-done) | data formatting | bytes 8388608
  170.4 0.0 copy-done.2
  170.4 0.6 copy.14
  171.0 0.0 copy-done.1
  171.0 0.6 copy.15
Async XLA Ops:
  163.5 4.9 %copy-start = (bf16[512,4096]{1,0:T(8,128)(2,1)S(1)}, bf16[512,4096]{1,0:T(8,128)(2,1)}, u32[]{:S(2)}) copy-start(bf16[512,4096]{1,0:T(8,128)(2,1)} %get-tuple-element.17) | copy-start | bytes 12582916
  168.4 2.0 %copy-start.2 = (f32[1,512]{1,0:T(1,128)S(1)}, f32[1,512]{1,0:T(1,128)}, u32[]{:S(2)}) copy-start(f32[1,512]{1,0:T(1,128)} %get-tuple-element.10) | copy-start | bytes 6148
  168.4 2.6 %copy-start.1 = (f32[1,512]{1,0:T(1,128)S(1)}, f32[1,512]{1,0:T(1,128)}, u32[]{:S(2)}) copy-start(f32[1,512]{1,0:T(1,128)} %get-tuple-element.11) | copy-start | bytes 6148

commit v4 on v3

--- a/solution.py
+++ b/solution.py
@@ -444,22 +444,39 @@
             stage.at[lax.rem(j, 2)], hbm.at[:, columns(j)], stage_sem.at[lax.rem(j, 2)]
         )
 
+    half = block // 2
+
+    def late_dot(side, start, j):
+        return jnp.dot(
+            weight[6 + side, :, start : start + half],
+            far[late[side], start : start + half, columns(j)],
+            preferred_element_type=jnp.float32,
+        )
+
+    def begin(side):
+        def first_half(j):
+            acc[side, j] += late_dot(side, 0, j)
+
+        loop(parts, first_half)
+
     def finish(side):
         def late_grad(j):
-            total = acc[side, j] + jnp.dot(
-                weight[6 + side], far[late[side], :, columns(j)], preferred_element_type=jnp.float32
-            )
+            total = acc[side, j] + late_dot(side, half, j)
 
             @pl.when(j >= 2)
             def _():
                 out_copy(side, j - 2).wait()
 
+            if side == 1:
+
+                @pl.when(j < 2)
+                def _():
+                    out_copy(0, parts - 2 + j).wait()
+
             stage[lax.rem(j, 2)] = (total * factor).astype(jnp.bfloat16)
             out_copy(side, j).start()
 
         loop(parts, late_grad)
-        out_copy(side, parts - 2).wait()
-        out_copy(side, parts - 1).wait()
 
     def forward(s):
         @pl.when(is_first)
@@ -475,28 +492,45 @@
 
     @pl.when(is_first)
     def _():
+        begin(0)
         finish(0)
 
-    for first, count in ((0, PIECES // 2), (PIECES // 2, 1), (PIECES // 2 + 1, 1)):
-        here = range(first, first + count)
-        if here[-1] == PIECES - 1:
-            forward(PIECES - 1)
+    def late_pieces(side, first, count):
+        if side == 1:
+            for s in range(first, first + count):
+                if s == PIECES - 1:
+                    forward(s)
 
         @pl.when(is_second)
         def _():
-            for s in here:
-                arrived(2, s)
-            weigh_late(0, first * rows, count * rows)
-            for s in here:
-                arrived(5, s)
-
-        weigh_late(1, first * rows, count * rows)
+            for s in range(first, first + count):
+                arrived(2 if side == 0 else 5, s)
+            if side == 0:
+                weigh_late(0, first * rows, count * rows)
+
+        if side == 1:
+            weigh_late(1, first * rows, count * rows)
+
+    late_pieces(0, 0, PIECES // 2)
+    late_pieces(1, 0, PIECES // 2)
 
     @pl.when(is_second)
     def _():
+        begin(0)
+
+    begin(1)
+    late_pieces(0, PIECES // 2, 1)
+    late_pieces(1, PIECES // 2, 1)
+    late_pieces(0, PIECES // 2 + 1, 1)
+
+    @pl.when(is_second)
+    def _():
         finish(0)
 
+    late_pieces(1, PIECES // 2 + 1, 1)
     finish(1)
+    out_copy(1, parts - 2).wait()
+    out_copy(1, parts - 1).wait()
 
     for k in range(3):
         flag_copy(k).wait_send()

time: 172 us -> 167 us (0.971)
  Pallas kernels: 163 us -> 158 us
    pallas_call x1, Pallas kernels: 163 us -> 158 us  [local(): pl.pallas_call(functools.partial(kernel, n), out_shape=(jax.ShapeDtypeStr...]
where the time goes in v4:
time: 167 us
  Pallas kernels  158 us (95%)
  local copies, waits for them, and re-layouts  8.03 us (5%)
    pallas_call x1, Pallas kernels, local(): pl.pallas_call(functools.partial(kernel, n), out_shape=(jax.ShapeDtypeStr...  158 us
    unnamed x10, local copies, waits for them, and re-layouts  8.03 us

profile of v4, /device:TPU:1, one launch (start us, length us, event | category | flops | bytes accessed | tf_op | source)
XLA Modules:
  0.0 166.6 jit_solution(14794350973883356564)
XLA Ops:
  0.6 157.9 %shard_map.75 = (bf16[512,4096]{1,0:T(8,128)(2,1)}, bf16[512,4096]{1,0:T(8,128)(2,1)}, f32[1,512]{1,0:T(1,128)}, f32[1,512]{1,0:T(1,128)}) custom-call(bf16[512,4096]{1,0:T(8,128)(2,1)} %q_hbm.1, bf16[512,4096]{1,0:T(8,128)(2,1)} %p_hbm.1, s32[1,3]{1,0:T(1,128)} %links_ref.1, s32[1,512]{1,0:T(1,128)} %pos_ref.1), custom_call_target="tpu_custom_call" | custom-call | flops 34359738368 | bytes 16777216 | tf_op jit(solution)/shard_map/pallas_call | solution.py:559
  158.6 0.0 copy-start
  158.6 4.8 %copy.12 = bf16[512,4096]{1,0:T(8,128)(2,1)} copy(bf16[512,4096]{1,0:T(8,128)(2,1)} %get-tuple-element.16) | data formatting | bytes 8388608
  163.4 0.0 copy-done
  163.4 0.0 copy-start.2
  163.4 0.0 copy-start.1
  163.4 2.0 %copy.13 = bf16[512,4096]{1,0:T(8,128)(2,1)} copy(bf16[512,4096]{1,0:T(8,128)(2,1)S(1)} %copy-done) | data formatting | bytes 8388608
  165.5 0.0 copy-done.2
  165.5 0.6 copy.14
  166.0 0.0 copy-done.1
  166.0 0.6 copy.15
Async XLA Ops:
  158.6 4.9 %copy-start = (bf16[512,4096]{1,0:T(8,128)(2,1)S(1)}, bf16[512,4096]{1,0:T(8,128)(2,1)}, u32[]{:S(2)}) copy-start(bf16[512,4096]{1,0:T(8,128)(2,1)} %get-tuple-element.17) | copy-start | bytes 12582916
  163.4 2.0 %copy-start.2 = (f32[1,512]{1,0:T(1,128)S(1)}, f32[1,512]{1,0:T(1,128)}, u32[]{:S(2)}) copy-start(f32[1,512]{1,0:T(1,128)} %get-tuple-element.10) | copy-start | bytes 6148
  163.4 2.6 %copy-start.1 = (f32[1,512]{1,0:T(1,128)S(1)}, f32[1,512]{1,0:T(1,128)}, u32[]{:S(2)}) copy-start(f32[1,512]{1,0:T(1,128)} %get-tuple-element.11) | copy-start | bytes 6148

commit v5 on v4

--- a/solution.py
+++ b/solution.py
@@ -19,8 +19,8 @@
     p_hbm,
     links_ref,
     pos_ref,
-    dq_hbm,
-    dp_hbm,
+    dq_ref,
+    dp_ref,
     row_ref,
     col_ref,
     own,
@@ -30,7 +30,6 @@
     top,
     mass,
     lse,
-    stage,
     upright,
     hit,
     said,
@@ -49,7 +48,6 @@
     flag_recv_sem,
     stat_send_sem,
     stat_recv_sem,
-    stage_sem,
 ):
     block, depth = q_hbm.shape
     factor = depth ** (-0.5)
@@ -176,7 +174,7 @@
         top[side] = now
 
     def tile(index, start, size):
-        per = stage.shape[2] // block
+        per = acc.shape[3] // block
         first = lax.rem(index, per) * block + start
         return (0, index // per, slice(None), pl.ds(pl.multiple_of(first, 128), size))
 
@@ -362,7 +360,7 @@
         return pl.ds(pl.multiple_of(i * STRIP, STRIP), STRIP)
 
     def weigh(side, index, theirs, i):
-        per = stage.shape[2] // block
+        per = acc.shape[3] // block
         at_tile = side * 3 + index if index < 3 else 6
         lanes = pl.ds(at_tile % per * block, block)
         score = acc[0, at_tile // per, strip(i), lanes]
@@ -408,7 +406,7 @@
     def _():
         loop(strips, lambda i: weigh(0, 3, heard[2, 0:1, :], i))
 
-    width = stage.shape[2]
+    width = acc.shape[3]
     parts = depth // width
 
     def columns(j):
@@ -438,12 +436,6 @@
         value = jnp.exp(part - lse[side, :, 0:1]) + jnp.exp(part - theirs)
         weight[6 + side, :, pl.ds(start, size)] = value.astype(jnp.bfloat16)
 
-    def out_copy(side, j):
-        hbm = dq_hbm if side == 0 else dp_hbm
-        return pltpu.make_async_copy(
-            stage.at[lax.rem(j, 2)], hbm.at[:, columns(j)], stage_sem.at[lax.rem(j, 2)]
-        )
-
     half = block // 2
 
     def late_dot(side, start, j):
@@ -463,18 +455,8 @@
         def late_grad(j):
             total = acc[side, j] + late_dot(side, half, j)
 
-            @pl.when(j >= 2)
-            def _():
-                out_copy(side, j - 2).wait()
-
-            if side == 1:
-
-                @pl.when(j < 2)
-                def _():
-                    out_copy(0, parts - 2 + j).wait()
-
-            stage[lax.rem(j, 2)] = (total * factor).astype(jnp.bfloat16)
-            out_copy(side, j).start()
+            out = dq_ref if side == 0 else dp_ref
+            out[:, columns(j)] = (total * factor).astype(jnp.bfloat16)
 
         loop(parts, late_grad)
 
@@ -529,8 +511,6 @@
 
     late_pieces(1, PIECES // 2 + 1, 1)
     finish(1)
-    out_copy(1, parts - 2).wait()
-    out_copy(1, parts - 1).wait()
 
     for k in range(3):
         flag_copy(k).wait_send()
@@ -559,10 +539,10 @@
     query_grad, passage_grad, row_loss, col_loss = pl.pallas_call(
         functools.partial(kernel, n),
         out_shape=(
-            jax.ShapeDtypeStruct((block, depth), jnp.bfloat16),
-            jax.ShapeDtypeStruct((block, depth), jnp.bfloat16),
-            jax.ShapeDtypeStruct((1, block), jnp.float32),
-            jax.ShapeDtypeStruct((1, block), jnp.float32),
+            pltpu.VMEM((block, depth), jnp.bfloat16),
+            pltpu.VMEM((block, depth), jnp.bfloat16),
+            pltpu.VMEM((1, block), jnp.float32),
+            pltpu.VMEM((1, block), jnp.float32),
         ),
         in_specs=[
             pl.BlockSpec(memory_space=pl.ANY),
@@ -571,8 +551,8 @@
             pl.BlockSpec(memory_space=pltpu.VMEM),
         ],
         out_specs=(
-            pl.BlockSpec(memory_space=pl.ANY),
-            pl.BlockSpec(memory_space=pl.ANY),
+            pl.BlockSpec(memory_space=pltpu.VMEM),
+            pl.BlockSpec(memory_space=pltpu.VMEM),
             pl.BlockSpec(memory_space=pltpu.VMEM),
             pl.BlockSpec(memory_space=pltpu.VMEM),
         ),
@@ -584,7 +564,6 @@
             pltpu.VMEM((2, block, 128), jnp.float32),
             pltpu.VMEM((2, block, 128), jnp.float32),
             pltpu.VMEM((2, block, 128), jnp.float32),
-            pltpu.VMEM((2, block, width), jnp.bfloat16),
             pltpu.VMEM((block, 128), jnp.float32),
             pltpu.VMEM((2, 8, block), jnp.float32),
             pltpu.VMEM((2, 8, block), jnp.float32),
@@ -603,13 +582,12 @@
             pltpu.SemaphoreType.DMA((3,)),
             pltpu.SemaphoreType.DMA((3,)),
             pltpu.SemaphoreType.DMA((2,)),
-            pltpu.SemaphoreType.DMA((2,)),
         ],
         cost_estimate=pl.CostEstimate(
             flops=flops, bytes_accessed=8 * block * depth, transcendentals=24 * block * block
         ),
         compiler_params=pltpu.CompilerParams(
-            collective_id=0, has_side_effects=True, vmem_limit_bytes=60 * 1024 * 1024
+            collective_id=0, has_side_effects=True, vmem_limit_bytes=55 * 1024 * 1024
         ),
     )(queries, passages, links, positives)
     return query_grad, passage_grad, row_loss.reshape(block), col_loss.reshape(block)

time: 167 us -> 161 us (0.964)
  Pallas kernels: 158 us -> 155 us
  local copies, waits for them, and re-layouts: 8.03 us -> 5.19 us
    unnamed x10 -> x4, local copies, waits for them, and re-layouts: 8.03 us -> 5.19 us
    pallas_call x1, Pallas kernels: 158 us -> 155 us  [local(): pl.pallas_call(functools.partial(kernel, n), out_shape=(pltpu.VMEM((block...]
where the time goes in v5:
time: 161 us
  Pallas kernels  155 us (96%)
  local copies, waits for them, and re-layouts  5.19 us (3%)
    pallas_call x1, Pallas kernels, local(): pl.pallas_call(functools.partial(kernel, n), out_shape=(pltpu.VMEM((block...  155 us
    unnamed x4, local copies, waits for them, and re-layouts  5.19 us

profile of v5, /device:TPU:1, one launch (start us, length us, event | category | flops | bytes accessed | tf_op | source)
XLA Modules:
  0.0 161.2 jit_solution(8681472466197947114)
XLA Ops:
  0.6 155.4 %shard_map.75 = (bf16[512,4096]{1,0:T(8,128)(2,1)S(1)}, bf16[512,4096]{1,0:T(8,128)(2,1)S(1)}, f32[1,512]{1,0:T(1,128)S(1)}, f32[1,512]{1,0:T(1,128)S(1)}) custom-call(bf16[512,4096]{1,0:T(8,128)(2,1)} %q_hbm.1, bf16[512,4096]{1,0:T(8,128)(2,1)} %p_hbm.1, s32[1,3]{1,0:T(1,128)} %links_ref.1, s32[1,512]{1,0:T(1,128)} %pos_ref.1), custom_call_target="tpu_custom_call" | custom-call | flops 34359738368 | bytes 16777216 | tf_op jit(solution)/shard_map/pallas_call | solution.py:539
  156.1 2.0 %copy.12 = bf16[512,4096]{1,0:T(8,128)(2,1)} copy(bf16[512,4096]{1,0:T(8,128)(2,1)S(1)} %get-tuple-element.12) | data formatting | bytes 8388608
  158.1 0.6 copy.14
  158.7 0.6 copy.15
  159.2 2.0 %copy.13 = bf16[512,4096]{1,0:T(8,128)(2,1)} copy(bf16[512,4096]{1,0:T(8,128)(2,1)S(1)} %get-tuple-element.13) | data formatting | bytes 8388608

commit v6 on v5

--- a/solution.py
+++ b/solution.py
@@ -501,15 +501,33 @@
         begin(0)
 
     begin(1)
-    late_pieces(0, PIECES // 2, 1)
-    late_pieces(1, PIECES // 2, 1)
-    late_pieces(0, PIECES // 2 + 1, 1)
-
-    @pl.when(is_second)
-    def _():
-        finish(0)
-
-    late_pieces(1, PIECES // 2 + 1, 1)
+    def last_piece(t):
+        side, s = lax.rem(t, 2), PIECES // 2 + t // 2
+
+        @pl.when(t == PIECES - 1)
+        def _():
+            forward(PIECES - 1)
+
+            @pl.when(is_second)
+            def _():
+                finish(0)
+
+        @pl.when(is_second)
+        def _():
+            arrived(2 + 3 * side, s)
+
+        @pl.when(is_second | (side == 1))
+        def _():
+            slot = 2 + side * (2 + second)
+            k = 3 - side * (1 - second)
+            part = dot_t(own[side], far[slot, piece(s), :]) * factor
+            flag = jnp.where(side == 0, flag_out[k - 1, 0:1, :], flag_in[k - 1, 0:1, :])[:, 0:1]
+            part = jnp.where(flag > 0, part, NEG)
+            theirs = heard[slot, 0:1, piece(s)]
+            value = jnp.exp(part - lse[side, :, 0:1]) + jnp.exp(part - theirs)
+            weight[6 + side, :, piece(s)] = value.astype(jnp.bfloat16)
+
+    loop(PIECES, last_piece)
     finish(1)
 
     for k in range(3):

time: 161 us -> 161 us (level)
  no operation moved by 1% of the time
where the time goes in v6:
time: 161 us
  Pallas kernels  155 us (96%)
  local copies, waits for them, and re-layouts  5.19 us (3%)
    pallas_call x1, Pallas kernels, local(): pl.pallas_call(functools.partial(kernel, n), out_shape=(pltpu.VMEM((block...  155 us
    unnamed x4, local copies, waits for them, and re-layouts  5.19 us

profile of v6, /device:TPU:1, one launch (start us, length us, event | category | flops | bytes accessed | tf_op | source)
XLA Modules:
  0.0 161.3 jit_solution(15667061133484688343)
XLA Ops:
  0.6 155.4 %shard_map.75 = (bf16[512,4096]{1,0:T(8,128)(2,1)S(1)}, bf16[512,4096]{1,0:T(8,128)(2,1)S(1)}, f32[1,512]{1,0:T(1,128)S(1)}, f32[1,512]{1,0:T(1,128)S(1)}) custom-call(bf16[512,4096]{1,0:T(8,128)(2,1)} %q_hbm.1, bf16[512,4096]{1,0:T(8,128)(2,1)} %p_hbm.1, s32[1,3]{1,0:T(1,128)} %links_ref.1, s32[1,512]{1,0:T(1,128)} %pos_ref.1), custom_call_target="tpu_custom_call" | custom-call | flops 34359738368 | bytes 16777216 | tf_op jit(solution)/shard_map/pallas_call | solution.py:557
  156.1 2.0 %copy.12 = bf16[512,4096]{1,0:T(8,128)(2,1)} copy(bf16[512,4096]{1,0:T(8,128)(2,1)S(1)} %get-tuple-element.12) | data formatting | bytes 8388608
  158.1 0.6 copy.14
  158.7 0.6 copy.15
  159.2 2.0 %copy.13 = bf16[512,4096]{1,0:T(8,128)(2,1)} copy(bf16[512,4096]{1,0:T(8,128)(2,1)S(1)} %get-tuple-element.13) | data formatting | bytes 8388608
